TPU v7x, 512 devices: a whole 4x4x16 slice. The times are simulated.
512 devices in a mesh: dp: 32 (over z_lo, x, core), fsdp: 16 (over y, z_hi).
Axes of the slice: x: 4, y: 4, z: 16 (z_hi: 4, z_lo: 4; z = z_hi * 4 + z_lo), core: 2. Of those that a mesh axis runs over, the one named last changes fastest.
Arguments:
- activations: bfloat16 [8192, 8192], P('dp', 'fsdp'), may hold values from -6 to 6
- out_cotangent: bfloat16 [8192, 28672], P('dp', 'fsdp'), may hold values from -6 to 6
- projector: bfloat16 [8192, 512], P('fsdp'), may hold values from -0.0625 to 0.0625
- first_moment: float32 [512, 28672], P('dp', 'fsdp'), may hold values from -4 to 4
- second_moment: float32 [512, 28672], P('dp', 'fsdp'), may hold values from 0.05 to 2
Outputs:
- new_first: float32 [512, 28672], P('dp', 'fsdp')
- new_second: float32 [512, 28672], P('dp', 'fsdp')
- weight_update: bfloat16 [28672, 8192], P('fsdp', 'dp')
All inputs are finite; a program needn't handle non-finite values.
Results may differ from a plain program's by a relative error of at most 0.017.
Values may be sent and summed in bfloat16 or wider, within the bound.
A program may use at most 64 MiB of HBM per device.

v0:
```python
import math

import jax
import jax.numpy as jnp
from jax import lax
from jax.sharding import PartitionSpec as P

STEP = 100


def adam_update(lowgrad, first_moment, second_moment):
    new_first = 0.9 * first_moment + (1.0 - 0.9) * lowgrad
    new_second = 0.999 * second_moment + (1.0 - 0.999) * lowgrad * lowgrad
    first_fix = 1.0 - 0.9**STEP
    second_fix = 1.0 - 0.999**STEP
    direction = (new_first / first_fix / (jnp.sqrt(new_second / second_fix) + 1e-08)).astype(
        jnp.bfloat16
    )
    return (new_first, new_second, direction)


def local(activations, out_cotangent, projector, first_moment, second_moment):
    dp_count = lax.axis_size("dp")
    dp_index = lax.axis_index("dp")
    total_tokens = activations.shape[0] * dp_count
    grad_scale = 1.0 / math.sqrt(total_tokens)
    contract_tokens = (((0,), (0,)), ((), ()))
    back_dims = (((0,), (1,)), ((), ()))
    partial_proj = jnp.dot(activations, projector, preferred_element_type=jnp.float32)
    projected = lax.psum(partial_proj.astype(jnp.bfloat16), "fsdp")
    rank_total = projected.shape[1]
    rank_share = rank_total // dp_count
    whole_basis = lax.all_gather(projector, "fsdp", axis=0, tiled=True)
    width_share = whole_basis.shape[0] // dp_count
    local_basis = lax.dynamic_slice_in_dim(whole_basis, dp_index * width_share, width_share, 0)
    local_grad = lax.dot_general(
        projected, out_cotangent, contract_tokens, preferred_element_type=jnp.float32
    )
    lowgrad = lax.psum(local_grad.astype(jnp.bfloat16), "dp").astype(jnp.float32) * grad_scale
    whole_first, whole_second = (
        lax.all_gather(first_moment, "dp", axis=0, tiled=True),
        lax.all_gather(second_moment, "dp", axis=0, tiled=True),
    )
    full_first, full_second, direction = adam_update(lowgrad, whole_first, whole_second)
    new_first = lax.dynamic_slice_in_dim(full_first, dp_index * rank_share, rank_share, 0)
    new_second = lax.dynamic_slice_in_dim(full_second, dp_index * rank_share, rank_share, 0)
    update = lax.dot_general(direction, local_basis, back_dims, preferred_element_type=jnp.float32)
    return (new_first, new_second, update.astype(jnp.bfloat16))


def solution(mesh):
    placed = (P("dp", "fsdp"), P("dp", "fsdp"), P("fsdp", None), P("dp", "fsdp"), P("dp", "fsdp"))
    return jax.shard_map(
        local,
        mesh=mesh,
        in_specs=placed,
        out_specs=(P("dp", "fsdp"), P("dp", "fsdp"), P("fsdp", "dp")),
        check_vma=False,
    )
```

profile of v0, /device:TPU:1, one launch (start us, length us, event | category | flops | bytes accessed | tf_op | source)
XLA Modules:
  0.0 877.3 jit_solution(17569797790506292644)
XLA Ops:
  7.2 0.0 copy-start
  7.2 0.0 all-reduce.3.cloned.1.call-start
  7.2 2.2 convolution_convert_fusion.2
  9.4 0.0 all-reduce.3.cloned.1.call-update
  9.4 0.0 all-reduce.5.cloned.1.call-start
  9.5 201.8 %all-reduce.3.cloned.1.call-done = bf16[256,512]{1,0:T(8,128)(2,1)} async-done(((bf16[256,512]{1,0:T(8,128)(2,1)}), bf16[256,512]{1,0:T(8,128)(2,1)}) %all-reduce.3.cloned.1.call-update) | async-done | bytes 262160 | tf_op jit(solution)/shard_map/psum | solution.py:30
  211.3 0.0 copy-done
  211.3 2.9 convolution_convert_fusion
  214.2 0.0 all-reduce.5.cloned.1.call-update
  214.2 0.0 all-gather.4.cloned.1.call-start
  214.3 0.7 all-gather.4.cloned.1.call-update
  215.0 0.0 all-gather.6.cloned.1.call-start
  215.0 0.5 all-gather.6.cloned.1.call-update
  215.6 0.0 all-gather.8.cloned.1.call-start
  215.6 0.5 all-gather.8.cloned.1.call-update
  216.1 294.0 %all-reduce.5.cloned.1.call-done = bf16[512,1792]{1,0:T(8,128)(2,1)} async-done(((bf16[512,1792]{1,0:T(8,128)(2,1)}), bf16[512,1792]{1,0:T(8,128)(2,1)}) %all-reduce.5.cloned.1.call-update) | async-done | bytes 1835024 | tf_op jit(solution)/shard_map/psum | solution.py:39
  510.2 68.8 %all-gather.4.cloned.1.call-done = f32[512,1792]{1,0:T(8,128)} async-done(((f32[16,1792]{1,0:T(8,128)}), f32[512,1792]{1,0:T(8,128)}) %all-gather.4.cloned.1.call-update) | async-done | bytes 3670032 | tf_op jit(solution)/shard_map/all_gather | solution.py:41
  579.0 68.4 %all-gather.6.cloned.1.call-done = f32[512,1792]{1,0:T(8,128)} async-done(((f32[16,1792]{1,0:T(8,128)}), f32[512,1792]{1,0:T(8,128)}) %all-gather.6.cloned.1.call-update) | async-done | bytes 3670032 | tf_op jit(solution)/shard_map/all_gather | solution.py:42
  647.4 4.9 fusion.2
  652.2 0.0 copy-start.1
  652.3 0.0 copy-start.2
  652.3 1.8 copy-done.1
  654.1 1.2 copy-done.2
  655.2 0.7 constant_dynamic-slice_fusion
  655.9 208.7 %all-gather.8.cloned.1.call-done = bf16[8192,512]{1,0:T(8,128)(2,1)} async-done(((bf16[512,512]{1,0:T(8,128)(2,1)}), bf16[8192,512]{1,0:T(8,128)(2,1)}) %all-gather.8.cloned.1.call-update) | async-done | bytes 8388624 | tf_op jit(solution)/shard_map/all_gather | solution.py:33
  864.7 6.1 convolution_convert_fusion.1
Async XLA Ops:
  7.2 204.2 %copy-start = (bf16[256,1792]{1,0:T(8,128)(2,1)S(1)}, bf16[256,1792]{1,0:T(8,128)(2,1)}, u32[]{:S(2)}) copy-start(bf16[256,1792]{1,0:T(8,128)(2,1)} %param.6) | copy-start | bytes 2752516
  7.2 204.2 %all-reduce.3.cloned.1.call-start = ((), (), s32[]{:S(2)}) async-start(), calls=%async_computation.1 | async-start | bytes 524288 | tf_op jit(solution)/shard_map/psum | solution.py:30
  9.4 500.8 %all-reduce.5.cloned.1.call-start = ((), (), s32[]{:S(2)}) async-start(), calls=%async_computation.2 | async-start | bytes 3670016 | tf_op jit(solution)/shard_map/psum | solution.py:39
  214.2 364.7 %all-gather.4.cloned.1.call-start = ((), (), s32[]{:S(2)}) async-start(), calls=%async_computation | async-start | bytes 3784704 | tf_op jit(solution)/shard_map/all_gather | solution.py:41
  215.0 432.4 %all-gather.6.cloned.1.call-start = ((), (), s32[]{:S(2)}) async-start(), calls=%async_computation.3 | async-start | bytes 3784704 | tf_op jit(solution)/shard_map/all_gather | solution.py:42
  215.6 649.1 %all-gather.8.cloned.1.call-start = ((), (), s32[]{:S(2)}) async-start(), calls=%async_computation.4 | async-start | bytes 8912896 | tf_op jit(solution)/shard_map/all_gather | solution.py:33
  652.2 1.8 copy-start.1
  652.3 3.0 copy-start.2
Sparse Core Ops, SparseCore 0:
  11.5 199.8 all-reduce.2
  214.5 295.6 all-reduce.4
  512.4 66.5 all-gather.3
  581.0 66.3 all-gather.5
  650.2 214.4 all-gather.7
where the time goes:
time: 877 us
  waiting for transfers between devices  844 us (96%)
  between operations  13.8 us (2%)
  matrix products  11.2 us (1%)
    psum x1, waiting for transfers between devices, local(): lax.psum(local_grad.astype(jnp.bfloat16), 'dp').astype(jnp.float32)  294 us
    all_gather x1, waiting for transfers between devices, local(): whole_basis = lax.all_gather(projector, 'fsdp', axis=0, tiled=True)  209 us
    psum x1, waiting for transfers between devices, local(): projected = lax.psum(partial_proj.astype(jnp.bfloat16), 'fsdp')  202 us
    all_gather x1, waiting for transfers between devices, local(): lax.all_gather(first_moment, 'dp', axis=0, tiled=True)  68.8 us
    all_gather x1, waiting for transfers between devices, local(): lax.all_gather(second_moment, 'dp', axis=0, tiled=True)  68.4 us
  transfers between devices with their start and end apart: 5, of which 5 were waited for; matrix products, arithmetic and copies ran while one was open for 1% of the time, Pallas kernels for 0%

commit v1 on v0

v1 whole, which is shorter than its diff:
```python
import functools
import math

import jax
import jax.numpy as jnp
from jax import lax
from jax.experimental import pallas as pl
from jax.experimental.pallas import tpu as pltpu
from jax.sharding import PartitionSpec as P

MESH = pl.DeviceIdType.MESH
STEP = 100
BF = jnp.bfloat16
F32 = jnp.float32
CHUNKS = ((0, 256), (256, 256), (512, 384))
N = 4


def adam(lowgrad, first, second):
    new_first = 0.9 * first + (1.0 - 0.9) * lowgrad
    new_second = 0.999 * second + (1.0 - 0.999) * lowgrad * lowgrad
    first_fix = 1.0 - 0.9**STEP
    second_fix = 1.0 - 0.999**STEP
    direction = new_first / first_fix / (jnp.sqrt(new_second / second_fix) + 1e-08)
    return new_first, new_second, direction.astype(BF)


def kernel(
    grad_scale, act_ref, cot_ref, proj_ref, m1_ref, m2_ref,
    nf_ref, ns_ref, up_ref,
    act, proj, cot_own, cot_sib, mom1, mom2, basis,
    part, y_in, y_sum, z_in, pj, pj_sib,
    lg, opp_l, opp_r, a_l, a_r, b_l, b_r, s2, zl_in,
    new1, new2, dirs, dirs_sib, upd,
    send_sems, recv_sems, local_sems,
):
    dp, fs = lax.axis_index("dp"), lax.axis_index("fsdp")
    zl, x, c = dp // 8, (dp // 2) % 4, dp % 2
    y, zh = fs // 4, fs % 4
    half = cot_own.shape[1]

    def dev(x=x, y=y, zh=zh, zl=zl, c=c):
        return (zl * 8 + x * 2 + c, y * 4 + zh)

    def at(base, off):
        return lax.rem(base + off, N)

    sibling = dev(c=1 - c)
    partner = dev(x=zh, y=zl, zh=x, zl=y)
    is_self = jnp.logical_and(x == zh, y == zl)
    counter = [0, 0]
    sent = []

    def remote(src, dst, device):
        i = counter[0]
        counter[0] += 1
        copy = pltpu.make_async_remote_copy(
            src_ref=src, dst_ref=dst, send_sem=send_sems.at[i], recv_sem=recv_sems.at[i],
            device_id=device, device_id_type=MESH,
        )
        return copy

    def go(src, dst, device):
        copy = remote(src, dst, device)
        copy.start()
        sent.append(copy)
        return copy

    def fetch(src, dst):
        i = counter[1]
        counter[1] += 1
        copy = pltpu.make_async_copy(src, dst, local_sems.at[i])
        copy.start()
        return copy

    own_cols = pl.ds(pl.multiple_of(c * half, 128), half)
    sib_cols = pl.ds(pl.multiple_of((1 - c) * half, 128), half)

    barrier = pltpu.get_barrier_semaphore()
    peers = [sibling]
    for o in (1, 2, 3):
        peers += [dev(y=at(y, o)), dev(zh=at(zh, o)), dev(x=at(x, o)), dev(zl=at(zl, o))]
    get_act = fetch(act_ref, act)
    get_proj = fetch(proj_ref, proj)
    for p in peers:
        pl.semaphore_signal(barrier, inc=1, device_id=p, device_id_type=MESH)

    @pl.when(jnp.logical_not(is_self))
    def _():
        pl.semaphore_signal(barrier, inc=1, device_id=partner, device_id_type=MESH)

    get_cot = fetch(cot_ref.at[:, own_cols], cot_own)
    get_m1 = fetch(m1_ref.at[:, own_cols], mom1.at[c])
    get_m2 = fetch(m2_ref.at[:, own_cols], mom2.at[c])

    get_act.wait()
    get_proj.wait()
    partial = jnp.dot(act[...], proj[...], preferred_element_type=F32)
    part[...] = jnp.transpose(partial).astype(BF).reshape(part.shape)

    pl.semaphore_wait(barrier, jnp.where(is_self, len(peers), len(peers) + 1))

    ys = [go(part.at[at(y, o)], y_in.at[o - 1], dev(y=at(y, o))) for o in (1, 2, 3)]
    cot_x = go(cot_ref.at[:, sib_cols], cot_sib, sibling)
    m1_x = go(m1_ref.at[:, sib_cols], mom1.at[c], sibling)
    m2_x = go(m2_ref.at[:, sib_cols], mom2.at[c], sibling)
    total = part[y].astype(F32)
    for o, copy in enumerate(ys):
        copy.wait_recv()
        total += y_in[o].astype(F32)
    y_sum[...] = total.astype(BF)
    zs = [go(y_sum.at[at(zh, o)], z_in.at[o - 1], dev(zh=at(zh, o))) for o in (1, 2, 3)]
    total = y_sum[zh].astype(F32)
    for o, copy in enumerate(zs):
        copy.wait_recv()
        total += z_in[o].astype(F32)
    pj[y, zh] = total.astype(BF)

    zg = [go(pj.at[y, zh], pj.at[y, zh], dev(zh=at(zh, o))) for o in (1, 2, 3)]
    for copy in zg:
        copy.wait_recv()
    yg = [go(pj.at[y], pj.at[y], dev(y=at(y, o))) for o in (1, 2, 3)]
    sib = [go(pj.at[y], pj_sib.at[y], sibling)]
    piece = basis.shape[1]
    rows = pl.ds(pl.multiple_of(c * (N * piece) + zl * piece, piece), piece)
    basis_x = remote(proj_ref.at[rows], basis.at[zl], partner)
    basis_own = pltpu.make_async_copy(proj_ref.at[rows], basis.at[zl], local_sems.at[counter[1]])
    counter[1] += 1

    @pl.when(is_self)
    def _():
        basis_own.start()

    @pl.when(jnp.logical_not(is_self))
    def _():
        basis_x.start()

    for o, copy in zip((1, 2, 3), yg):
        copy.wait_recv()
        yy = at(y, N - o)
        sib.append(go(pj.at[yy], pj_sib.at[yy], sibling))
    get_cot.wait()
    cot_x.wait_recv()
    for copy in sib:
        copy.wait_recv()

    right, left = at(x, 1), at(x, 3)
    opposite = at(x, 2)
    to_right, to_left = dev(x=right), dev(x=left)
    low, high = pl.ds(0, 2), pl.ds(2, 2)
    flight = [dict() for _ in CHUNKS]

    def produce(k):
        start, width = CHUNKS[k]
        cols = pl.ds(start, width)
        f = flight[k]
        grad = jnp.dot(
            pj[...].reshape(N * N * 32, -1), cot_own[:, cols], preferred_element_type=F32
        ) + jnp.dot(
            pj_sib[...].reshape(N * N * 32, -1), cot_sib[:, cols], preferred_element_type=F32
        )
        lg[:, :, :, cols] = grad.astype(BF).reshape(N, N, 32, width)
        f["opp_l"] = go(lg.at[low, opposite, :, cols], opp_l.at[:, :, cols], to_right)
        f["opp_r"] = go(lg.at[high, opposite, :, cols], opp_r.at[:, :, cols], to_left)
        f["b_l"] = go(lg.at[high, right, :, cols], b_l.at[:, :, cols], to_right)
        f["a_r"] = go(lg.at[low, left, :, cols], a_r.at[:, :, cols], to_left)

    def pass_on(k):
        start, width = CHUNKS[k]
        cols = pl.ds(start, width)
        f = flight[k]
        f["opp_l"].wait_recv()
        lg[0:2, right, :, cols] = (
            lg[0:2, right, :, cols].astype(F32) + opp_l[:, :, cols].astype(F32)
        ).astype(BF)
        f["a_l"] = go(lg.at[low, right, :, cols], a_l.at[:, :, cols], to_right)
        f["opp_r"].wait_recv()
        lg[2:4, left, :, cols] = (
            lg[2:4, left, :, cols].astype(F32) + opp_r[:, :, cols].astype(F32)
        ).astype(BF)
        f["b_r"] = go(lg.at[high, left, :, cols], b_r.at[:, :, cols], to_left)

    def sum_x(k):
        start, width = CHUNKS[k]
        cols = pl.ds(start, width)
        f = flight[k]
        f["a_l"].wait_recv()
        f["a_r"].wait_recv()
        s2[0:2, :, cols] = (
            lg[0:2, x, :, cols].astype(F32) + a_l[:, :, cols].astype(F32)
            + a_r[:, :, cols].astype(F32)
        ).astype(BF)
        f["b_l"].wait_recv()
        f["b_r"].wait_recv()
        s2[2:4, :, cols] = (
            lg[2:4, x, :, cols].astype(F32) + b_l[:, :, cols].astype(F32)
            + b_r[:, :, cols].astype(F32)
        ).astype(BF)
        f["zl"] = [
            go(s2.at[at(zl, o), :, cols], zl_in.at[o - 1, :, cols], dev(zl=at(zl, o)))
            for o in (1, 2, 3)
        ]

    def step(k):
        start, width = CHUNKS[k]
        cols = pl.ds(start, width)
        f = flight[k]
        if k == 0:
            get_m1.wait()
            get_m2.wait()
            m1_x.wait_recv()
            m2_x.wait_recv()
        total = s2[zl, :, cols].astype(F32)
        for o, copy in enumerate(f["zl"]):
            copy.wait_recv()
            total += zl_in[o, :, cols].astype(F32)
        lowgrad = (total * grad_scale).reshape(2, 16, width)
        first, second, direction = adam(lowgrad, mom1[:, :, cols], mom2[:, :, cols])
        dirs[zl, x, :, cols] = direction.reshape(32, width)
        f["zg"] = [
            go(dirs.at[zl, x, :, cols], dirs.at[zl, x, :, cols], dev(zl=at(zl, o)))
            for o in (1, 2, 3)
        ]
        new1[:, :, cols] = first
        new2[:, :, cols] = second

    def send_x(k):
        start, width = CHUNKS[k]
        cols = pl.ds(start, width)
        f = flight[k]
        for copy in f["zg"]:
            copy.wait_recv()
        src_a, src_b = dirs.at[low, x, :, cols], dirs.at[high, x, :, cols]
        f["ga_l"] = go(src_a, src_a, to_right)
        f["gb_r"] = go(src_b, src_b, to_left)
        f["gb_l"] = go(src_b, src_b, to_right)
        f["ga_r"] = go(src_a, src_a, to_left)
        every = pl.ds(0, N)
        f["sib"] = [go(dirs.at[every, x, :, cols], dirs_sib.at[every, x, :, cols], sibling)]

    def forward_x(k):
        start, width = CHUNKS[k]
        cols = pl.ds(start, width)
        f = flight[k]
        every = pl.ds(0, N)
        f["ga_l"].wait_recv()
        src = dirs.at[low, left, :, cols]
        f["oa"] = go(src, src, to_right)
        f["gb_r"].wait_recv()
        src = dirs.at[high, right, :, cols]
        f["ob"] = go(src, src, to_left)
        f["gb_l"].wait_recv()
        f["sib"].append(
            go(dirs.at[every, left, :, cols], dirs_sib.at[every, left, :, cols], sibling)
        )
        f["ga_r"].wait_recv()
        f["sib"].append(
            go(dirs.at[every, right, :, cols], dirs_sib.at[every, right, :, cols], sibling)
        )

    def last_x(k):
        start, width = CHUNKS[k]
        cols = pl.ds(start, width)
        f = flight[k]
        every = pl.ds(0, N)
        f["oa"].wait_recv()
        f["ob"].wait_recv()
        f["sib"].append(
            go(dirs.at[every, opposite, :, cols], dirs_sib.at[every, opposite, :, cols], sibling)
        )

    back = (((0,), (1,)), ((), ()))
    written = []

    def update(k):
        start, width = CHUNKS[k]
        cols = pl.ds(start, width)
        f = flight[k]
        whole = basis[...].reshape(N * piece, -1)
        for j, (ref, core) in enumerate(((dirs, c), (dirs_sib, 1 - c))):
            if j == 1:
                for copy in f["sib"]:
                    copy.wait_recv()
            d = ref[:, :, :, cols].reshape(N * N * 32, width)
            upd[j, cols] = lax.dot_general(
                d, whole, back, preferred_element_type=F32
            ).astype(BF)
            written.append(
                fetch(
                    upd.at[j, cols],
                    up_ref.at[pl.ds(pl.multiple_of(core * half + start, 128), width)],
                )
            )

    def basis_round():
        @pl.when(is_self)
        def _():
            basis_own.wait()

        @pl.when(jnp.logical_not(is_self))
        def _():
            basis_x.wait_recv()

        return [go(basis.at[y], basis.at[y], dev(y=at(y, o))) for o in (1, 2, 3)]

    stages = (produce, pass_on, sum_x, step, send_x, forward_x, last_x, update)
    moments_out = None
    for t in range(len(CHUNKS) + len(stages) - 1):
        for s in reversed(range(len(stages))):
            k = t - s
            if 0 <= k < len(CHUNKS):
                if s == 2 and k == 0:
                    basis_copies = basis_round()
                if s == 7 and k == 0:
                    for copy in basis_copies:
                        copy.wait_recv()
                stages[s](k)
                if s == 3 and k == len(CHUNKS) - 1:
                    moments_out = [
                        go(new1.at[1 - c], nf_ref.at[:, own_cols], sibling),
                        go(new2.at[1 - c], ns_ref.at[:, own_cols], sibling),
                    ]
                    written.append(fetch(new1.at[c], nf_ref.at[:, own_cols]))
                    written.append(fetch(new2.at[c], ns_ref.at[:, own_cols]))
    for copy in moments_out:
        copy.wait_recv()
    for copy in written:
        copy.wait()
    for copy in sent:
        copy.wait_send()

    @pl.when(jnp.logical_not(is_self))
    def _():
        basis_x.wait_send()


def local(activations, out_cotangent, projector, first_moment, second_moment):
    tokens, features = activations.shape
    ff = out_cotangent.shape[1]
    rank = projector.shape[1]
    half = ff // 2
    total_tokens = tokens * lax.axis_size("dp")
    width = projector.shape[0] // 2
    block = (2, 32, half)
    remotes = 3 + 1 + 3 * 5 + 3 + 3 + 2 + len(CHUNKS) * (6 + 3 + 3 + 6 + 4)
    locals_ = 8 + 2 * len(CHUNKS)
    vmem = pltpu.VMEM
    scratch = [
        vmem((tokens, features), BF), vmem(projector.shape, BF),
        vmem((tokens, half), BF), vmem((tokens, half), BF),
        vmem((2, 16, half), F32), vmem((2, 16, half), F32),
        vmem((N, width // N, rank), BF),
        vmem((N, N, 32, tokens), BF), vmem((3, N, 32, tokens), BF), vmem((N, 32, tokens), BF),
        vmem((3, 32, tokens), BF), vmem((N, N, 32, tokens), BF), vmem((N, N, 32, tokens), BF),
        vmem((N, N, 32, half), BF),
        vmem(block, BF), vmem(block, BF), vmem(block, BF), vmem(block, BF),
        vmem(block, BF), vmem(block, BF),
        vmem((N, 32, half), BF), vmem((3, 32, half), BF),
        vmem((2, 16, half), F32), vmem((2, 16, half), F32),
        vmem((N, N, 32, half), BF), vmem((N, N, 32, half), BF),
        vmem((2, half, width), BF),
        pltpu.SemaphoreType.DMA((remotes,)), pltpu.SemaphoreType.DMA((remotes,)),
        pltpu.SemaphoreType.DMA((locals_,)),
    ]
    anyspec = pl.BlockSpec(memory_space=pl.ANY)
    return pl.pallas_call(
        functools.partial(kernel, 1.0 / math.sqrt(total_tokens)),
        out_shape=(
            jax.ShapeDtypeStruct(first_moment.shape, F32),
            jax.ShapeDtypeStruct(second_moment.shape, F32),
            jax.ShapeDtypeStruct((ff, width), BF),
        ),
        in_specs=[anyspec] * 5,
        out_specs=(anyspec,) * 3,
        scratch_shapes=scratch,
        compiler_params=pltpu.CompilerParams(
            collective_id=0, has_side_effects=True, vmem_limit_bytes=48 * 1024 * 1024
        ),
    )(activations, out_cotangent, projector, first_moment, second_moment)


def solution(mesh):
    placed = (P("dp", "fsdp"), P("dp", "fsdp"), P("fsdp", None), P("dp", "fsdp"), P("dp", "fsdp"))
    return jax.shard_map(
        local,
        mesh=mesh,
        in_specs=placed,
        out_specs=(P("dp", "fsdp"), P("dp", "fsdp"), P("fsdp", "dp")),
        check_vma=False,
    )
```

time: 877 us -> 89 us (0.10)
  waiting for transfers between devices: 844 us -> 0 us
  Pallas kernels: 0 us -> 80.9 us
  between operations: 13.8 us -> 0.65 us
  matrix products: 11.2 us -> 0 us
    psum x2 -> x0, waiting for transfers between devices: 496 us -> none  [the longest x1 294 us: local(): lax.psum(local_grad.astype(jnp.bfloat16), 'dp').astype(jnp.float32)]
    all_gather x3 -> x0, waiting for transfers between devices: 346 us -> none  [the longest x1 209 us: local(): whole_basis = lax.all_gather(projector, 'fsdp', axis=0, tiled=True)]
    pallas_call x0 -> x1, Pallas kernels: none -> 80.9 us  [local(): pl.pallas_call(functools.partial(kernel, 1.0 / math.sqrt(total_tokens)),...]
    dot_general x3 -> x0, matrix products: 11.2 us -> none  [the longest x1 6.1 us: local(): lax.dot_general(direction, local_basis, back_dims, preferred_element_type...]
  transfers between devices with their start and end apart: 5 -> 0, of which waited for: 5 -> 0; matrix products, arithmetic and copies ran while one was open for 1% -> 0% of each run, Pallas kernels for 0% -> 0%
where the time goes in v1:
time: 89 us; the launch traced here: 88.7 us
  Pallas kernels  80.9 us (91%)
  local copies, waits for them, and re-layouts  7.17 us (8%)
    pallas_call x1, Pallas kernels, local(): pl.pallas_call(functools.partial(kernel, 1.0 / math.sqrt(total_tokens)),...  80.9 us
    unnamed x13, local copies, waits for them, and re-layouts  7.17 us

profile of v1, /device:TPU:1, one launch (start us, length us, event | category | flops | bytes accessed | tf_op | source)
XLA Modules:
  0.0 88.7 jit_solution(11344758931503912768)
XLA Ops:
  0.6 0.0 copy-start
  0.6 1.2 %copy-done = bf16[256,1792]{1,0:T(8,128)(2,1)S(1)} copy-done((bf16[256,1792]{1,0:T(8,128)(2,1)S(1)}, bf16[256,1792]{1,0:T(8,128)(2,1)}, u32[]{:S(2)}) %copy-start) | copy-done | bytes 917528
  1.8 0.0 copy-start.1
  1.8 1.0 %copy-done.1 = bf16[512,512]{1,0:T(8,128)(2,1)S(1)} copy-done((bf16[512,512]{1,0:T(8,128)(2,1)S(1)}, bf16[512,512]{1,0:T(8,128)(2,1)}, u32[]{:S(2)}) %copy-start.1) | copy-done | bytes 524312
  2.9 0.0 copy-start.2
  2.9 0.9 %copy-done.2 = bf16[256,512]{1,0:T(8,128)(2,1)S(1)} copy-done((bf16[256,512]{1,0:T(8,128)(2,1)S(1)}, bf16[256,512]{1,0:T(8,128)(2,1)}, u32[]{:S(2)}) %copy-start.2) | copy-done | bytes 262168
  3.8 0.0 copy-start.3
  3.8 0.9 %copy-done.3 = f32[16,1792]{1,0:T(8,128)S(1)} copy-done((f32[16,1792]{1,0:T(8,128)S(1)}, f32[16,1792]{1,0:T(8,128)}, u32[]{:S(2)}) %copy-start.3) | copy-done | bytes 114712
  4.7 0.0 copy-start.4
  4.7 0.9 %copy-done.4 = f32[16,1792]{1,0:T(8,128)S(1)} copy-done((f32[16,1792]{1,0:T(8,128)S(1)}, f32[16,1792]{1,0:T(8,128)}, u32[]{:S(2)}) %copy-start.4) | copy-done | bytes 114712
  5.6 80.9 %shard_map.76 = (f32[16,1792]{1,0:T(8,128)S(1)}, f32[16,1792]{1,0:T(8,128)S(1)}, bf16[1792,256]{1,0:T(8,128)(2,1)S(1)}) custom-call(bf16[256,512]{1,0:T(8,128)(2,1)S(1)} %copy-done.2, bf16[256,1792]{1,0:T(8,128)(2,1)S(1)} %copy-done, bf16[512,512]{1,0:T(8,128)(2,1)S(1)} %copy-done.1, f32[16,1792]{1,0:T(8,128)S(1)} %copy-done.3, f32[16,1792]{1,0:T(8,128)S(1)} %copy-done.4), custom_call_target="tpu_custom_call" | custom-call | tf_op jit(solution)/shard_map/pallas_call | solution.py:366
  86.5 0.6 copy.11
  87.2 0.6 copy.12
  87.8 0.9 %copy.13 = bf16[1792,256]{1,0:T(8,128)(2,1)} copy(bf16[1792,256]{1,0:T(8,128)(2,1)S(1)} %get-tuple-element.8) | data formatting | bytes 1835008
Async XLA Ops:
  0.6 1.2 %copy-start = (bf16[256,1792]{1,0:T(8,128)(2,1)S(1)}, bf16[256,1792]{1,0:T(8,128)(2,1)}, u32[]{:S(2)}) copy-start(bf16[256,1792]{1,0:T(8,128)(2,1)} %cot_ref.1) | copy-start | bytes 2752516
  1.8 1.0 %copy-start.1 = (bf16[512,512]{1,0:T(8,128)(2,1)S(1)}, bf16[512,512]{1,0:T(8,128)(2,1)}, u32[]{:S(2)}) copy-start(bf16[512,512]{1,0:T(8,128)(2,1)} %proj_ref.1) | copy-start | bytes 1572868
  2.9 0.9 %copy-start.2 = (bf16[256,512]{1,0:T(8,128)(2,1)S(1)}, bf16[256,512]{1,0:T(8,128)(2,1)}, u32[]{:S(2)}) copy-start(bf16[256,512]{1,0:T(8,128)(2,1)} %act_ref.1) | copy-start | bytes 786436
  3.8 0.9 %copy-start.3 = (f32[16,1792]{1,0:T(8,128)S(1)}, f32[16,1792]{1,0:T(8,128)}, u32[]{:S(2)}) copy-start(f32[16,1792]{1,0:T(8,128)} %m1_ref.1) | copy-start | bytes 344068
  4.7 0.9 %copy-start.4 = (f32[16,1792]{1,0:T(8,128)S(1)}, f32[16,1792]{1,0:T(8,128)}, u32[]{:S(2)}) copy-start(f32[16,1792]{1,0:T(8,128)} %m2_ref.1) | copy-start | bytes 344068

commit v2 on v0

v2 whole, which is shorter than its diff:
```python
import functools
import math

import jax
import jax.numpy as jnp
from jax import lax
from jax.experimental import pallas as pl
from jax.experimental.pallas import tpu as pltpu
from jax.sharding import PartitionSpec as P

MESH = pl.DeviceIdType.MESH
STEP = 100
BF = jnp.bfloat16
F32 = jnp.float32
CHUNKS = ((0, 256), (256, 256), (512, 384))
N = 4
ORDER = (2, 1, 3, 0)


def adam(lowgrad, first, second):
    new_first = 0.9 * first + (1.0 - 0.9) * lowgrad
    new_second = 0.999 * second + (1.0 - 0.999) * lowgrad * lowgrad
    first_fix = 1.0 - 0.9**STEP
    second_fix = 1.0 - 0.999**STEP
    direction = new_first / first_fix / (jnp.sqrt(new_second / second_fix) + 1e-08)
    return new_first, new_second, direction.astype(BF)


def kernel(
    grad_scale, act_ref, cot_ref, proj_ref, m1_ref, m2_ref,
    nf_ref, ns_ref, up_ref,
    act, proj, cot_own, cot_sib, mom1, mom2, basis, quarter, turned,
    part, y_in, y_sum, z_in, pj, pj_sib,
    lg, g_in, s2, zl_in, new1, new2, dirs, dirs_sib, upd,
    send_sems, recv_sems, local_sems,
):
    dp, fs = lax.axis_index("dp"), lax.axis_index("fsdp")
    zl, x, c = dp // 8, (dp // 2) % 4, dp % 2
    y, zh = fs // 4, fs % 4
    half = cot_own.shape[1]

    def dev(x=x, y=y, zh=zh, zl=zl, c=c):
        return (zl * 8 + x * 2 + c, y * 4 + zh)

    def at(base, off):
        return lax.rem(base + off, N)

    sibling = dev(c=1 - c)
    root = y == zl
    turn = at(x, zl)
    goal = lax.rem(zh - x - zl + 2 * N, N)
    turns, moves = turn != 0, goal != x
    counter = [0, 0]
    sent = []

    def remote(src, dst, device, recv=None):
        i = counter[0]
        counter[0] += 1
        copy = pltpu.make_async_remote_copy(
            src_ref=src, dst_ref=dst, send_sem=send_sems.at[i],
            recv_sem=recv_sems.at[i if recv is None else recv],
            device_id=device, device_id_type=MESH,
        )
        return copy

    def go(src, dst, device):
        copy = remote(src, dst, device)
        copy.start()
        sent.append(copy)
        return copy

    def held(src, dst):
        i = counter[1]
        counter[1] += 1
        return pltpu.make_async_copy(src, dst, local_sems.at[i])

    def fetch(src, dst):
        copy = held(src, dst)
        copy.start()
        return copy

    own_cols = pl.ds(pl.multiple_of(c * half, 128), half)
    sib_cols = pl.ds(pl.multiple_of((1 - c) * half, 128), half)

    barrier = pltpu.get_barrier_semaphore()
    peers = [sibling]
    for o in (1, 2, 3):
        peers += [dev(y=at(y, o)), dev(zh=at(zh, o)), dev(x=at(x, o)), dev(zl=at(zl, o))]
    get_act = fetch(act_ref, act)
    get_proj = fetch(proj_ref, proj)
    for p in peers:
        pl.semaphore_signal(barrier, inc=1, device_id=p, device_id_type=MESH)

    get_cot = fetch(cot_ref.at[:, own_cols], cot_own)
    get_m1 = fetch(m1_ref.at[:, own_cols], mom1.at[c])
    get_m2 = fetch(m2_ref.at[:, own_cols], mom2.at[c])

    get_act.wait()
    get_proj.wait()
    partial = jnp.dot(act[...], proj[...], preferred_element_type=F32)
    part[...] = jnp.transpose(partial).astype(BF).reshape(part.shape)

    pl.semaphore_wait(barrier, len(peers))
    pieces = [at(x, o) for o in ORDER]
    ys = [
        [go(part.at[at(y, o), p], y_in.at[o - 1, p], dev(y=at(y, o))) for o in (2, 1, 3)]
        for p in pieces
    ]
    cot_x = go(cot_ref.at[:, sib_cols], cot_sib, sibling)
    m1_x = go(m1_ref.at[:, sib_cols], mom1.at[c], sibling)
    m2_x = go(m2_ref.at[:, sib_cols], mom2.at[c], sibling)
    zs = []
    for p, copies in zip(pieces, ys):
        for copy in copies:
            copy.wait_recv()
        total = part[y, p].astype(F32)
        for o in range(3):
            total += y_in[o, p].astype(F32)
        y_sum[p] = total.astype(BF)
        zs.append(
            [go(y_sum.at[p], z_in.at[o - 1, p], dev(zh=at(zh, o))) for o in (2, 1, 3)]
        )

    piece = basis.shape[1]

    def rows(q):
        return proj_ref.at[pl.ds(pl.multiple_of(c * (N * piece) + q * piece, piece), piece)]

    first_sem = counter[0]
    basis_cut = [
        remote(rows(at(y, o)), quarter, dev(y=at(y, o)), first_sem) for o in (1, 2, 3)
    ]
    basis_own = held(rows(y), quarter)

    @pl.when(root)
    def _():
        for basis_part in basis_cut:
            basis_part.start()
        basis_own.start()

    handed = [None] * N
    relayed = [None] * N
    grads = [[] for _ in CHUNKS]

    def add_z(i):
        p = pieces[i]
        for copy in zs[i]:
            copy.wait_recv()
        total = y_sum[p].astype(F32)
        for o in range(3):
            total += z_in[o, p].astype(F32)
        pj[y, p] = total.astype(BF)
        handed[i] = [go(pj.at[y, p], pj.at[y, p], dev(y=at(y, o))) for o in (2, 1, 3)]
        relayed[i] = [go(pj.at[y, p], pj_sib.at[y, p], sibling)]

    def relay(i):
        p = pieces[i]
        for o, copy in zip((2, 1, 3), handed[i]):
            copy.wait_recv()
            yy = at(y, N - o)
            relayed[i].append(go(pj.at[yy, p], pj_sib.at[yy, p], sibling))

    def multiply(i):
        p, o = pieces[i], ORDER[i]
        if i == 0:
            get_cot.wait()
            cot_x.wait_recv()
        for copy in relayed[i]:
            copy.wait_recv()
        grad = jnp.dot(
            pj[:, p].reshape(N * 32, -1), cot_own[...], preferred_element_type=F32
        ) + jnp.dot(pj_sib[:, p].reshape(N * 32, -1), cot_sib[...], preferred_element_type=F32)
        lg[p] = grad.astype(BF).reshape(N, 32, half)
        if o:
            for k, (start, width) in enumerate(CHUNKS):
                cols = pl.ds(start, width)
                grads[k].append(
                    go(lg.at[p, :, :, cols], g_in.at[o - 1, :, :, cols], dev(x=p))
                )

    basis_turn = remote(quarter, turned, dev(zh=at(zh, turn)))
    basis_stay = held(quarter, turned)
    basis_move = remote(turned, basis.at[y], dev(x=goal))
    basis_keep = held(turned, basis.at[y])

    def turn_basis(i):
        @pl.when(root)
        def _():
            basis_own.wait()

        @pl.when(jnp.logical_not(root))
        def _():
            basis_cut[0].wait_recv()

        @pl.when(turns)
        def _():
            basis_turn.start()

        @pl.when(jnp.logical_not(turns))
        def _():
            basis_stay.start()

    def move_basis():
        @pl.when(turns)
        def _():
            basis_turn.wait_recv()

        @pl.when(jnp.logical_not(turns))
        def _():
            basis_stay.wait()

        @pl.when(moves)
        def _():
            basis_move.start()

        @pl.when(jnp.logical_not(moves))
        def _():
            basis_keep.start()

    def share_basis():
        @pl.when(moves)
        def _():
            basis_move.wait_recv()

        @pl.when(jnp.logical_not(moves))
        def _():
            basis_keep.wait()

        return [go(basis.at[y], basis.at[y], dev(y=at(y, o))) for o in (1, 2, 3)]

    for act_on, i in (
        (add_z, 0), (add_z, 1), (relay, 0), (multiply, 0), (add_z, 2), (relay, 1), (multiply, 1),
        (add_z, 3), (turn_basis, 0), (relay, 2), (multiply, 2), (relay, 3), (multiply, 3),
    ):
        act_on(i)

    flight = [dict() for _ in CHUNKS]

    def sum_x(k):
        start, width = CHUNKS[k]
        cols = pl.ds(start, width)
        for copy in grads[k]:
            copy.wait_recv()
        total = lg[x, :, :, cols].astype(F32)
        for o in range(3):
            total += g_in[o, :, :, cols].astype(F32)
        s2[:, :, cols] = total.astype(BF)
        flight[k]["zl"] = [
            go(s2.at[at(zl, o), :, cols], zl_in.at[o - 1, :, cols], dev(zl=at(zl, o)))
            for o in (1, 2, 3)
        ]

    def step(k):
        start, width = CHUNKS[k]
        cols = pl.ds(start, width)
        f = flight[k]
        if k == 0:
            get_m1.wait()
            get_m2.wait()
            m1_x.wait_recv()
            m2_x.wait_recv()
        for copy in f["zl"]:
            copy.wait_recv()
        total = s2[zl, :, cols].astype(F32)
        for o in range(3):
            total += zl_in[o, :, cols].astype(F32)
        lowgrad = (total * grad_scale).reshape(2, 16, width)
        first, second, direction = adam(lowgrad, mom1[:, :, cols], mom2[:, :, cols])
        dirs[zl, x, :, cols] = direction.reshape(32, width)
        src = dirs.at[zl, x, :, cols]
        f["zg"] = [go(src, src, dev(zl=at(zl, o))) for o in (1, 2, 3)]
        new1[:, :, cols] = first
        new2[:, :, cols] = second

    def block(ref, k, p):
        start, width = CHUNKS[k]
        return ref.at[pl.ds(0, N), p, :, pl.ds(start, width)]

    def send_x(k):
        f = flight[k]
        for copy in f["zg"]:
            copy.wait_recv()
        src = block(dirs, k, x)
        f["xg"] = [go(src, src, dev(x=at(x, o))) for o in (2, 1, 3)]
        f["sib"] = [go(src, block(dirs_sib, k, x), sibling)]

    def relay_x(k):
        f = flight[k]
        for o, copy in zip((2, 1, 3), f["xg"]):
            copy.wait_recv()
            xx = at(x, N - o)
            f["sib"].append(go(block(dirs, k, xx), block(dirs_sib, k, xx), sibling))

    back = (((0,), (1,)), ((), ()))
    written = []

    def update(k):
        start, width = CHUNKS[k]
        cols = pl.ds(start, width)
        if k == 0:
            for copy in basis_copies:
                copy.wait_recv()
        whole = basis[...].reshape(N * piece, -1)
        for j, (ref, core) in enumerate(((dirs, c), (dirs_sib, 1 - c))):
            if j == 1:
                for copy in flight[k]["sib"]:
                    copy.wait_recv()
            d = ref[:, :, :, cols].reshape(N * N * 32, width)
            upd[j, cols] = lax.dot_general(
                d, whole, back, preferred_element_type=F32
            ).astype(BF)
            written.append(
                fetch(
                    upd.at[j, cols],
                    up_ref.at[pl.ds(pl.multiple_of(core * half + start, 128), width)],
                )
            )

    def each(act_on):
        for k in range(len(CHUNKS)):
            act_on(k)

    each(sum_x)
    move_basis()
    each(step)
    moments_out = [
        go(new1.at[1 - c], nf_ref.at[:, own_cols], sibling),
        go(new2.at[1 - c], ns_ref.at[:, own_cols], sibling),
    ]
    written.append(fetch(new1.at[c], nf_ref.at[:, own_cols]))
    written.append(fetch(new2.at[c], ns_ref.at[:, own_cols]))
    send_x(0)
    basis_copies = share_basis()
    for k in range(1, len(CHUNKS)):
        send_x(k)
    for k in range(len(CHUNKS)):
        relay_x(k)
        update(k)
    assert counter[0] <= send_sems.shape[0] and counter[1] <= local_sems.shape[0]
    for copy in moments_out:
        copy.wait_recv()
    for copy in written:
        copy.wait()
    for copy in sent:
        copy.wait_send()

    @pl.when(root)
    def _():
        for basis_part in basis_cut:
            basis_part.wait_send()

    @pl.when(turns)
    def _():
        basis_turn.wait_send()

    @pl.when(moves)
    def _():
        basis_move.wait_send()


def hand_over(a_ref, b_ref, c_ref, a_out, b_out, c_out, a, b, c, sems):
    rows = c.shape[0] // 4
    trips = [(a_ref, a, a_out), (b_ref, b, b_out)]
    for i in range(4):
        part = pl.ds(i * rows, rows)
        trips.append((c_ref.at[part], c.at[part], c_out.at[part]))
    inward = [pltpu.make_async_copy(s, v, sems.at[0, i]) for i, (s, v, _) in enumerate(trips)]
    outward = [pltpu.make_async_copy(v, d, sems.at[1, i]) for i, (_, v, d) in enumerate(trips)]
    for copy in inward:
        copy.start()
    for arrive, leave in zip(inward, outward):
        arrive.wait()
        leave.start()
    for copy in outward:
        copy.wait()


def local(activations, out_cotangent, projector, first_moment, second_moment):
    tokens, features = activations.shape
    ff = out_cotangent.shape[1]
    rank = projector.shape[1]
    half = ff // 2
    width = projector.shape[0] // 2
    total_tokens = tokens * lax.axis_size("dp")
    remotes = 12 + 3 + 12 + N * 7 + 8 + len(CHUNKS) * (3 + 3 + 3 + 3 + 4) + 2
    locals_ = 10 + 2 * len(CHUNKS)
    vmem = pltpu.VMEM
    scratch = [
        vmem((tokens, features), BF), vmem(projector.shape, BF),
        vmem((tokens, half), BF), vmem((tokens, half), BF),
        vmem((2, 16, half), F32), vmem((2, 16, half), F32),
        vmem((N, width // N, rank), BF), vmem((width // N, rank), BF), vmem((width // N, rank), BF),
        vmem((N, N, 32, tokens), BF), vmem((3, N, 32, tokens), BF), vmem((N, 32, tokens), BF),
        vmem((3, N, 32, tokens), BF), vmem((N, N, 32, tokens), BF), vmem((N, N, 32, tokens), BF),
        vmem((N, N, 32, half), BF), vmem((3, N, 32, half), BF),
        vmem((N, 32, half), BF), vmem((3, 32, half), BF),
        vmem((2, 16, half), F32), vmem((2, 16, half), F32),
        vmem((N, N, 32, half), BF), vmem((N, N, 32, half), BF),
        vmem((2, half, width), BF),
        pltpu.SemaphoreType.DMA((remotes,)), pltpu.SemaphoreType.DMA((remotes,)),
        pltpu.SemaphoreType.DMA((locals_,)),
    ]
    anyspec = pl.BlockSpec(memory_space=pl.ANY)
    outs = (
        jax.ShapeDtypeStruct(first_moment.shape, F32),
        jax.ShapeDtypeStruct(second_moment.shape, F32),
        jax.ShapeDtypeStruct((ff, width), BF),
    )
    results = pl.pallas_call(
        functools.partial(kernel, 1.0 / math.sqrt(total_tokens)),
        out_shape=outs,
        in_specs=[anyspec] * 5,
        out_specs=(anyspec,) * 3,
        scratch_shapes=scratch,
        compiler_params=pltpu.CompilerParams(
            collective_id=0, has_side_effects=True, vmem_limit_bytes=56 * 1024 * 1024
        ),
    )(activations, out_cotangent, projector, first_moment, second_moment)
    return pl.pallas_call(
        hand_over,
        out_shape=outs,
        in_specs=[anyspec] * 3,
        out_specs=(anyspec,) * 3,
        scratch_shapes=[vmem(o.shape, o.dtype) for o in outs]
        + [pltpu.SemaphoreType.DMA((2, 6))],
        compiler_params=pltpu.CompilerParams(vmem_limit_bytes=56 * 1024 * 1024),
    )(*results)


def solution(mesh):
    placed = (P("dp", "fsdp"), P("dp", "fsdp"), P("fsdp", None), P("dp", "fsdp"), P("dp", "fsdp"))
    return jax.shard_map(
        local,
        mesh=mesh,
        in_specs=placed,
        out_specs=(P("dp", "fsdp"), P("dp", "fsdp"), P("fsdp", "dp")),
        check_vma=False,
    )
```

time: 877 us -> 72.2 us (0.08)
  waiting for transfers between devices: 844 us -> 0 us
  Pallas kernels: 0 us -> 71.4 us
  between operations: 13.8 us -> 0.64 us
  matrix products: 11.2 us -> 0 us
    psum x2 -> x0, waiting for transfers between devices: 496 us -> none  [the longest x1 294 us: local(): lax.psum(local_grad.astype(jnp.bfloat16), 'dp').astype(jnp.float32)]
    all_gather x3 -> x0, waiting for transfers between devices: 346 us -> none  [the longest x1 209 us: local(): whole_basis = lax.all_gather(projector, 'fsdp', axis=0, tiled=True)]
    pallas_call x0 -> x2, Pallas kernels: none -> 71.4 us  [the longest x1 69.3 us: local(): pl.pallas_call(functools.partial(kernel, 1.0 / math.sqrt(total_tokens)),...]
    dot_general x3 -> x0, matrix products: 11.2 us -> none  [the longest x1 6.1 us: local(): lax.dot_general(direction, local_basis, back_dims, preferred_element_type...]
  transfers between devices with their start and end apart: 5 -> 0, of which waited for: 5 -> 0; matrix products, arithmetic and copies ran while one was open for 1% -> 0% of each run, Pallas kernels for 0% -> 0%
where the time goes in v2:
time: 72.2 us; the launch traced here: 72 us
  Pallas kernels  71.4 us (99%)
    pallas_call x1, Pallas kernels, local(): pl.pallas_call(functools.partial(kernel, 1.0 / math.sqrt(total_tokens)),...  69.3 us
    pallas_call x1, Pallas kernels, local(): pl.pallas_call(hand_over, out_shape=outs, in_specs=[anyspec] * 3, out_spe...  2.14 us

profile of v2, /device:TPU:1, one launch (start us, length us, event | category | flops | bytes accessed | tf_op | source)
XLA Modules:
  0.0 72.0 jit_solution(18426956063953496054)
XLA Ops:
  0.6 69.3 %shard_map.76 = (f32[16,1792]{1,0:T(8,128)}, f32[16,1792]{1,0:T(8,128)}, bf16[1792,256]{1,0:T(8,128)(2,1)}) custom-call(bf16[256,512]{1,0:T(8,128)(2,1)} %act_ref.1, bf16[256,1792]{1,0:T(8,128)(2,1)} %cot_ref.1, bf16[512,512]{1,0:T(8,128)(2,1)} %proj_ref.1, f32[16,1792]{1,0:T(8,128)} %m1_ref.1, f32[16,1792]{1,0:T(8,128)} %m2_ref.1), custom_call_target="tpu_custom_call" | custom-call | tf_op jit(solution)/shard_map/pallas_call | solution.py:409
  69.9 2.1 %shard_map.77 = (f32[16,1792]{1,0:T(8,128)}, f32[16,1792]{1,0:T(8,128)}, bf16[1792,256]{1,0:T(8,128)(2,1)}) custom-call(f32[16,1792]{1,0:T(8,128)} %get-tuple-element.6.a_ref, f32[16,1792]{1,0:T(8,128)} %get-tuple-element.7.b_ref, bf16[1792,256]{1,0:T(8,128)(2,1)} %get-tuple-element.8.c_ref), custom_call_target="tpu_custom_call" | custom-call | tf_op jit(solution)/shard_map/pallas_call | solution.py:419

commit v3 on v2

--- a/solution.py
+++ b/solution.py
@@ -14,7 +14,8 @@
 F32 = jnp.float32
 CHUNKS = ((0, 256), (256, 256), (512, 384))
 N = 4
-ORDER = (2, 1, 3, 0)
+PIECES = ((2, 0, 32), (1, 0, 32), (3, 0, 32), (0, 0, 32))
+DIRECT = (0, 1, 2)
 
 
 def adam(lowgrad, first, second):
@@ -32,7 +33,7 @@
     act, proj, cot_own, cot_sib, mom1, mom2, basis, quarter, turned,
     part, y_in, y_sum, z_in, pj, pj_sib,
     lg, g_in, s2, zl_in, new1, new2, dirs, dirs_sib, upd,
-    send_sems, recv_sems, local_sems,
+    send_sems, recv_sems, local_sems, opposite_in,
 ):
     dp, fs = lax.axis_index("dp"), lax.axis_index("fsdp")
     zl, x, c = dp // 8, (dp // 2) % 4, dp % 2
@@ -83,9 +84,10 @@
     sib_cols = pl.ds(pl.multiple_of((1 - c) * half, 128), half)
 
     barrier = pltpu.get_barrier_semaphore()
-    peers = [sibling]
-    for o in (1, 2, 3):
-        peers += [dev(y=at(y, o)), dev(zh=at(zh, o)), dev(x=at(x, o)), dev(zl=at(zl, o))]
+    far = (2, 1, 3)
+    peers = [dev(zh=at(zh, o)) for o in (1, 3)] + [dev(y=at(y, o)) for o in far] + [sibling]
+    peers += [dev(y=at(y, o), c=1 - c) for o in far]
+    peers += [dev(zl=at(zl, o)) for o in far] + [dev(x=at(x, o)) for o in far]
     get_act = fetch(act_ref, act)
     get_proj = fetch(proj_ref, proj)
     for p in peers:
@@ -101,25 +103,29 @@
     part[...] = jnp.transpose(partial).astype(BF).reshape(part.shape)
 
     pl.semaphore_wait(barrier, len(peers))
-    pieces = [at(x, o) for o in ORDER]
+    pl.semaphore_signal(opposite_in, inc=1, device_id=dev(zh=at(zh, 1)), device_id_type=MESH)
+    pieces = [(at(x, o), pl.ds(start, count)) for o, start, count in PIECES]
     ys = [
-        [go(part.at[at(y, o), p], y_in.at[o - 1, p], dev(y=at(y, o))) for o in (2, 1, 3)]
-        for p in pieces
+        [go(part.at[at(y, o), p, r], y_in.at[o - 1, p, r], dev(y=at(y, o))) for o in far]
+        for p, r in pieces
     ]
     cot_x = go(cot_ref.at[:, sib_cols], cot_sib, sibling)
     m1_x = go(m1_ref.at[:, sib_cols], mom1.at[c], sibling)
     m2_x = go(m2_ref.at[:, sib_cols], mom2.at[c], sibling)
     zs = []
-    for p, copies in zip(pieces, ys):
+    for (p, r), copies in zip(pieces, ys):
         for copy in copies:
             copy.wait_recv()
-        total = part[y, p].astype(F32)
+        total = part[y, p, r].astype(F32)
         for o in range(3):
-            total += y_in[o, p].astype(F32)
-        y_sum[p] = total.astype(BF)
-        zs.append(
-            [go(y_sum.at[p], z_in.at[o - 1, p], dev(zh=at(zh, o))) for o in (2, 1, 3)]
-        )
+            total += y_in[o, p, r].astype(F32)
+        y_sum[p, r] = total.astype(BF)
+        copies = []
+        for o in far if zs else (1, 3, 2):
+            if o == 2 and not zs:
+                pl.semaphore_wait(opposite_in, 1)
+            copies.append(go(y_sum.at[p, r], z_in.at[o - 1, p, r], dev(zh=at(zh, o))))
+        zs.append(copies)
 
     piece = basis.shape[1]
 
@@ -138,44 +144,41 @@
             basis_part.start()
         basis_own.start()
 
-    handed = [None] * N
-    relayed = [None] * N
+    handed = [None] * len(PIECES)
     grads = [[] for _ in CHUNKS]
 
     def add_z(i):
-        p = pieces[i]
+        p, r = pieces[i]
         for copy in zs[i]:
             copy.wait_recv()
-        total = y_sum[p].astype(F32)
+        total = y_sum[p, r].astype(F32)
         for o in range(3):
-            total += z_in[o, p].astype(F32)
-        pj[y, p] = total.astype(BF)
-        handed[i] = [go(pj.at[y, p], pj.at[y, p], dev(y=at(y, o))) for o in (2, 1, 3)]
-        relayed[i] = [go(pj.at[y, p], pj_sib.at[y, p], sibling)]
-
-    def relay(i):
-        p = pieces[i]
-        for o, copy in zip((2, 1, 3), handed[i]):
-            copy.wait_recv()
-            yy = at(y, N - o)
-            relayed[i].append(go(pj.at[yy, p], pj_sib.at[yy, p], sibling))
+            total += z_in[o, p, r].astype(F32)
+        pj[y, p, r] = total.astype(BF)
+        src = pj.at[y, p, r]
+        handed[i] = [go(src, src, dev(y=at(y, o))) for o in far]
+        handed[i] += [go(src, pj_sib.at[y, p, r], dev(y=at(y, o), c=1 - c)) for o in far]
+        handed[i].append(go(src, pj_sib.at[y, p, r], sibling))
 
     def multiply(i):
-        p, o = pieces[i], ORDER[i]
+        p, r = pieces[i]
+        o, begin, count = PIECES[i]
         if i == 0:
             get_cot.wait()
             cot_x.wait_recv()
-        for copy in relayed[i]:
+        for copy in handed[i]:
             copy.wait_recv()
         grad = jnp.dot(
-            pj[:, p].reshape(N * 32, -1), cot_own[...], preferred_element_type=F32
-        ) + jnp.dot(pj_sib[:, p].reshape(N * 32, -1), cot_sib[...], preferred_element_type=F32)
-        lg[p] = grad.astype(BF).reshape(N, 32, half)
+            pj[:, p, r].reshape(N * count, -1), cot_own[...], preferred_element_type=F32
+        ) + jnp.dot(
+            pj_sib[:, p, r].reshape(N * count, -1), cot_sib[...], preferred_element_type=F32
+        )
+        lg[p, :, r] = grad.astype(BF).reshape(N, count, half)
         if o:
             for k, (start, width) in enumerate(CHUNKS):
                 cols = pl.ds(start, width)
                 grads[k].append(
-                    go(lg.at[p, :, :, cols], g_in.at[o - 1, :, :, cols], dev(x=p))
+                    go(lg.at[p, :, r, cols], g_in.at[o - 1, :, r, cols], dev(x=p))
                 )
 
     basis_turn = remote(quarter, turned, dev(zh=at(zh, turn)))
@@ -229,8 +232,8 @@
         return [go(basis.at[y], basis.at[y], dev(y=at(y, o))) for o in (1, 2, 3)]
 
     for act_on, i in (
-        (add_z, 0), (add_z, 1), (relay, 0), (multiply, 0), (add_z, 2), (relay, 1), (multiply, 1),
-        (add_z, 3), (turn_basis, 0), (relay, 2), (multiply, 2), (relay, 3), (multiply, 3),
+        (add_z, 0), (add_z, 1), (multiply, 0), (add_z, 2), (multiply, 1), (add_z, 3),
+        (turn_basis, 0), (multiply, 2), (multiply, 3),
     ):
         act_on(i)
 
@@ -281,15 +284,28 @@
         for copy in f["zg"]:
             copy.wait_recv()
         src = block(dirs, k, x)
-        f["xg"] = [go(src, src, dev(x=at(x, o))) for o in (2, 1, 3)]
+        f["xg"] = {o: go(src, src, dev(x=at(x, o))) for o in (far if k in DIRECT else (1, 3))}
         f["sib"] = [go(src, block(dirs_sib, k, x), sibling)]
 
+    def to_sibling(k, o):
+        xx = at(x, N - o)
+        flight[k]["sib"].append(go(block(dirs, k, xx), block(dirs_sib, k, xx), sibling))
+
     def relay_x(k):
+        start, width = CHUNKS[k]
         f = flight[k]
-        for o, copy in zip((2, 1, 3), f["xg"]):
-            copy.wait_recv()
-            xx = at(x, N - o)
-            f["sib"].append(go(block(dirs, k, xx), block(dirs_sib, k, xx), sibling))
+        for o in (1, 3):
+            f["xg"][o].wait_recv()
+            if k not in DIRECT:
+                src = dirs.at[pl.ds(o - 1, 2), at(x, N - o), :, pl.ds(start, width)]
+                f["xg"][4 + o] = go(src, src, dev(x=at(x, o)))
+            to_sibling(k, o)
+
+    def finish_x(k):
+        f = flight[k]
+        for o in (2,) if k in DIRECT else (5, 7):
+            f["xg"][o].wait_recv()
+        to_sibling(k, 2)
 
     back = (((0,), (1,)), ((), ()))
     written = []
@@ -333,9 +349,11 @@
     basis_copies = share_basis()
     for k in range(1, len(CHUNKS)):
         send_x(k)
-    for k in range(len(CHUNKS)):
-        relay_x(k)
-        update(k)
+    for act_on, k in (
+        (relay_x, 0), (relay_x, 1), (finish_x, 0), (update, 0), (finish_x, 1), (relay_x, 2),
+        (finish_x, 2), (update, 1), (update, 2),
+    ):
+        act_on(k)
     assert counter[0] <= send_sems.shape[0] and counter[1] <= local_sems.shape[0]
     for copy in moments_out:
         copy.wait_recv()
@@ -382,7 +400,7 @@
     half = ff // 2
     width = projector.shape[0] // 2
     total_tokens = tokens * lax.axis_size("dp")
-    remotes = 12 + 3 + 12 + N * 7 + 8 + len(CHUNKS) * (3 + 3 + 3 + 3 + 4) + 2
+    remotes = 13 * len(PIECES) + 3 + 8 + len(CHUNKS) * (len(PIECES) - 1 + 3 + 3 + 8) + 2
     locals_ = 10 + 2 * len(CHUNKS)
     vmem = pltpu.VMEM
     scratch = [
@@ -398,7 +416,7 @@
         vmem((N, N, 32, half), BF), vmem((N, N, 32, half), BF),
         vmem((2, half, width), BF),
         pltpu.SemaphoreType.DMA((remotes,)), pltpu.SemaphoreType.DMA((remotes,)),
-        pltpu.SemaphoreType.DMA((locals_,)),
+        pltpu.SemaphoreType.DMA((locals_,)), pltpu.SemaphoreType.REGULAR,
     ]
     anyspec = pl.BlockSpec(memory_space=pl.ANY)
     outs = (

time: 72.2 us -> 72.1 us (level)
  no operation moved by 1% of the time
where the time goes in v3:
time: 72.1 us; the launch traced here: 71.9 us
  Pallas kernels  71.3 us (99%)
    pallas_call x1, Pallas kernels, local(): pl.pallas_call(functools.partial(kernel, 1.0 / math.sqrt(total_tokens)),...  69.1 us
    pallas_call x1, Pallas kernels, local(): pl.pallas_call(hand_over, out_shape=outs, in_specs=[anyspec] * 3, out_spe...  2.14 us

profile of v3, /device:TPU:1, one launch (start us, length us, event | category | flops | bytes accessed | tf_op | source)
XLA Modules:
  0.0 71.9 jit_solution(8726169019787496315)
XLA Ops:
  0.6 69.1 %shard_map.76 = (f32[16,1792]{1,0:T(8,128)}, f32[16,1792]{1,0:T(8,128)}, bf16[1792,256]{1,0:T(8,128)(2,1)}) custom-call(bf16[256,512]{1,0:T(8,128)(2,1)} %act_ref.1, bf16[256,1792]{1,0:T(8,128)(2,1)} %cot_ref.1, bf16[512,512]{1,0:T(8,128)(2,1)} %proj_ref.1, f32[16,1792]{1,0:T(8,128)} %m1_ref.1, f32[16,1792]{1,0:T(8,128)} %m2_ref.1), custom_call_target="tpu_custom_call" | custom-call | tf_op jit(solution)/shard_map/pallas_call | solution.py:427
  69.8 2.1 %shard_map.77 = (f32[16,1792]{1,0:T(8,128)}, f32[16,1792]{1,0:T(8,128)}, bf16[1792,256]{1,0:T(8,128)(2,1)}) custom-call(f32[16,1792]{1,0:T(8,128)} %get-tuple-element.6.a_ref, f32[16,1792]{1,0:T(8,128)} %get-tuple-element.7.b_ref, bf16[1792,256]{1,0:T(8,128)(2,1)} %get-tuple-element.8.c_ref), custom_call_target="tpu_custom_call" | custom-call | tf_op jit(solution)/shard_map/pallas_call | solution.py:437

commit v4 on v3

--- a/solution.py
+++ b/solution.py
@@ -15,7 +15,6 @@
 CHUNKS = ((0, 256), (256, 256), (512, 384))
 N = 4
 PIECES = ((2, 0, 32), (1, 0, 32), (3, 0, 32), (0, 0, 32))
-DIRECT = (0, 1, 2)
 
 
 def adam(lowgrad, first, second):
@@ -33,7 +32,7 @@
     act, proj, cot_own, cot_sib, mom1, mom2, basis, quarter, turned,
     part, y_in, y_sum, z_in, pj, pj_sib,
     lg, g_in, s2, zl_in, new1, new2, dirs, dirs_sib, upd,
-    send_sems, recv_sems, local_sems, opposite_in,
+    send_sems, recv_sems, local_sems,
 ):
     dp, fs = lax.axis_index("dp"), lax.axis_index("fsdp")
     zl, x, c = dp // 8, (dp // 2) % 4, dp % 2
@@ -85,7 +84,7 @@
 
     barrier = pltpu.get_barrier_semaphore()
     far = (2, 1, 3)
-    peers = [dev(zh=at(zh, o)) for o in (1, 3)] + [dev(y=at(y, o)) for o in far] + [sibling]
+    peers = [dev(zh=at(zh, o)) for o in far] + [dev(y=at(y, o)) for o in far] + [sibling]
     peers += [dev(y=at(y, o), c=1 - c) for o in far]
     peers += [dev(zl=at(zl, o)) for o in far] + [dev(x=at(x, o)) for o in far]
     get_act = fetch(act_ref, act)
@@ -103,7 +102,6 @@
     part[...] = jnp.transpose(partial).astype(BF).reshape(part.shape)
 
     pl.semaphore_wait(barrier, len(peers))
-    pl.semaphore_signal(opposite_in, inc=1, device_id=dev(zh=at(zh, 1)), device_id_type=MESH)
     pieces = [(at(x, o), pl.ds(start, count)) for o, start, count in PIECES]
     ys = [
         [go(part.at[at(y, o), p, r], y_in.at[o - 1, p, r], dev(y=at(y, o))) for o in far]
@@ -120,12 +118,7 @@
         for o in range(3):
             total += y_in[o, p, r].astype(F32)
         y_sum[p, r] = total.astype(BF)
-        copies = []
-        for o in far if zs else (1, 3, 2):
-            if o == 2 and not zs:
-                pl.semaphore_wait(opposite_in, 1)
-            copies.append(go(y_sum.at[p, r], z_in.at[o - 1, p, r], dev(zh=at(zh, o))))
-        zs.append(copies)
+        zs.append([go(y_sum.at[p, r], z_in.at[o - 1, p, r], dev(zh=at(zh, o))) for o in far])
 
     piece = basis.shape[1]
 
@@ -284,7 +277,7 @@
         for copy in f["zg"]:
             copy.wait_recv()
         src = block(dirs, k, x)
-        f["xg"] = {o: go(src, src, dev(x=at(x, o))) for o in (far if k in DIRECT else (1, 3))}
+        f["xg"] = {o: go(src, src, dev(x=at(x, o))) for o in far}
         f["sib"] = [go(src, block(dirs_sib, k, x), sibling)]
 
     def to_sibling(k, o):
@@ -292,19 +285,13 @@
         flight[k]["sib"].append(go(block(dirs, k, xx), block(dirs_sib, k, xx), sibling))
 
     def relay_x(k):
-        start, width = CHUNKS[k]
         f = flight[k]
         for o in (1, 3):
             f["xg"][o].wait_recv()
-            if k not in DIRECT:
-                src = dirs.at[pl.ds(o - 1, 2), at(x, N - o), :, pl.ds(start, width)]
-                f["xg"][4 + o] = go(src, src, dev(x=at(x, o)))
             to_sibling(k, o)
 
     def finish_x(k):
-        f = flight[k]
-        for o in (2,) if k in DIRECT else (5, 7):
-            f["xg"][o].wait_recv()
+        flight[k]["xg"][2].wait_recv()
         to_sibling(k, 2)
 
     back = (((0,), (1,)), ((), ()))
@@ -400,7 +387,7 @@
     half = ff // 2
     width = projector.shape[0] // 2
     total_tokens = tokens * lax.axis_size("dp")
-    remotes = 13 * len(PIECES) + 3 + 8 + len(CHUNKS) * (len(PIECES) - 1 + 3 + 3 + 8) + 2
+    remotes = 13 * len(PIECES) + 3 + 8 + len(CHUNKS) * (len(PIECES) - 1 + 3 + 3 + 7) + 2
     locals_ = 10 + 2 * len(CHUNKS)
     vmem = pltpu.VMEM
     scratch = [
@@ -416,7 +403,7 @@
         vmem((N, N, 32, half), BF), vmem((N, N, 32, half), BF),
         vmem((2, half, width), BF),
         pltpu.SemaphoreType.DMA((remotes,)), pltpu.SemaphoreType.DMA((remotes,)),
-        pltpu.SemaphoreType.DMA((locals_,)), pltpu.SemaphoreType.REGULAR,
+        pltpu.SemaphoreType.DMA((locals_,)),
     ]
     anyspec = pl.BlockSpec(memory_space=pl.ANY)
     outs = (

time: 72.1 us -> 71.3 us (0.989)
  Pallas kernels: 71.3 us -> 70.5 us
    pallas_call x1, Pallas kernels: 69.1 us -> 68.4 us  [local(): pl.pallas_call(functools.partial(kernel, 1.0 / math.sqrt(total_tokens)),...]
where the time goes in v4:
time: 71.3 us; the launch traced here: 71.1 us
  Pallas kernels  70.5 us (99%)
    pallas_call x1, Pallas kernels, local(): pl.pallas_call(functools.partial(kernel, 1.0 / math.sqrt(total_tokens)),...  68.4 us
    pallas_call x1, Pallas kernels, local(): pl.pallas_call(hand_over, out_shape=outs, in_specs=[anyspec] * 3, out_spe...  2.14 us

profile of v4, /device:TPU:1, one launch (start us, length us, event | category | flops | bytes accessed | tf_op | source)
XLA Modules:
  0.0 71.1 jit_solution(10748810498459682376)
XLA Ops:
  0.6 68.4 %shard_map.76 = (f32[16,1792]{1,0:T(8,128)}, f32[16,1792]{1,0:T(8,128)}, bf16[1792,256]{1,0:T(8,128)(2,1)}) custom-call(bf16[256,512]{1,0:T(8,128)(2,1)} %act_ref.1, bf16[256,1792]{1,0:T(8,128)(2,1)} %cot_ref.1, bf16[512,512]{1,0:T(8,128)(2,1)} %proj_ref.1, f32[16,1792]{1,0:T(8,128)} %m1_ref.1, f32[16,1792]{1,0:T(8,128)} %m2_ref.1), custom_call_target="tpu_custom_call" | custom-call | tf_op jit(solution)/shard_map/pallas_call | solution.py:414
  69.0 2.1 %shard_map.77 = (f32[16,1792]{1,0:T(8,128)}, f32[16,1792]{1,0:T(8,128)}, bf16[1792,256]{1,0:T(8,128)(2,1)}) custom-call(f32[16,1792]{1,0:T(8,128)} %get-tuple-element.6.a_ref, f32[16,1792]{1,0:T(8,128)} %get-tuple-element.7.b_ref, bf16[1792,256]{1,0:T(8,128)(2,1)} %get-tuple-element.8.c_ref), custom_call_target="tpu_custom_call" | custom-call | tf_op jit(solution)/shard_map/pallas_call | solution.py:424

commit v5 on v4

--- a/solution.py
+++ b/solution.py
@@ -149,8 +149,10 @@
             total += z_in[o, p, r].astype(F32)
         pj[y, p, r] = total.astype(BF)
         src = pj.at[y, p, r]
-        handed[i] = [go(src, src, dev(y=at(y, o))) for o in far]
-        handed[i] += [go(src, pj_sib.at[y, p, r], dev(y=at(y, o), c=1 - c)) for o in far]
+        handed[i] = []
+        for o in far:
+            handed[i].append(go(src, pj_sib.at[y, p, r], dev(y=at(y, o), c=1 - c)))
+            handed[i].append(go(src, src, dev(y=at(y, o))))
         handed[i].append(go(src, pj_sib.at[y, p, r], sibling))
 
     def multiply(i):
@@ -243,7 +245,7 @@
         s2[:, :, cols] = total.astype(BF)
         flight[k]["zl"] = [
             go(s2.at[at(zl, o), :, cols], zl_in.at[o - 1, :, cols], dev(zl=at(zl, o)))
-            for o in (1, 2, 3)
+            for o in far
         ]
 
     def step(k):
@@ -264,7 +266,7 @@
         first, second, direction = adam(lowgrad, mom1[:, :, cols], mom2[:, :, cols])
         dirs[zl, x, :, cols] = direction.reshape(32, width)
         src = dirs.at[zl, x, :, cols]
-        f["zg"] = [go(src, src, dev(zl=at(zl, o))) for o in (1, 2, 3)]
+        f["zg"] = [go(src, src, dev(zl=at(zl, o))) for o in far]
         new1[:, :, cols] = first
         new2[:, :, cols] = second
 

time: 71.3 us -> 70.8 us (level)
  no operation moved by 1% of the time
where the time goes in v5:
time: 70.8 us; the launch traced here: 70.7 us
  Pallas kernels  70 us (99%)
    pallas_call x1, Pallas kernels, local(): pl.pallas_call(functools.partial(kernel, 1.0 / math.sqrt(total_tokens)),...  67.9 us
    pallas_call x1, Pallas kernels, local(): pl.pallas_call(hand_over, out_shape=outs, in_specs=[anyspec] * 3, out_spe...  2.14 us

profile of v5, /device:TPU:1, one launch (start us, length us, event | category | flops | bytes accessed | tf_op | source)
XLA Modules:
  0.0 70.7 jit_solution(1466295082382872748)
XLA Ops:
  0.6 67.9 %shard_map.76 = (f32[16,1792]{1,0:T(8,128)}, f32[16,1792]{1,0:T(8,128)}, bf16[1792,256]{1,0:T(8,128)(2,1)}) custom-call(bf16[256,512]{1,0:T(8,128)(2,1)} %act_ref.1, bf16[256,1792]{1,0:T(8,128)(2,1)} %cot_ref.1, bf16[512,512]{1,0:T(8,128)(2,1)} %proj_ref.1, f32[16,1792]{1,0:T(8,128)} %m1_ref.1, f32[16,1792]{1,0:T(8,128)} %m2_ref.1), custom_call_target="tpu_custom_call" | custom-call | tf_op jit(solution)/shard_map/pallas_call | solution.py:416
  68.5 2.1 %shard_map.77 = (f32[16,1792]{1,0:T(8,128)}, f32[16,1792]{1,0:T(8,128)}, bf16[1792,256]{1,0:T(8,128)(2,1)}) custom-call(f32[16,1792]{1,0:T(8,128)} %get-tuple-element.6.a_ref, f32[16,1792]{1,0:T(8,128)} %get-tuple-element.7.b_ref, bf16[1792,256]{1,0:T(8,128)(2,1)} %get-tuple-element.8.c_ref), custom_call_target="tpu_custom_call" | custom-call | tf_op jit(solution)/shard_map/pallas_call | solution.py:426
